TPU v7x, 32 devices: a whole 2x2x4 slice. The times are simulated.
32 devices in a mesh: row: 16 (over z, y, x), rhs: 2 (over core).
Axes of the slice: x: 2, y: 2, z: 4, core: 2. Of those that a mesh axis runs over, the one named last changes fastest.
Arguments:
- right_sides: float32 [64, 8, 1024], P('rhs', None, 'row'), parts along dimension 0, may hold values from -6 to 6
- lower_blocks: float32 [28, 1024, 1024], P(None, 'row'), may hold values from -0.078125 to 0.078125
- inverse_blocks: float32 [8, 1024, 1024], P(None, 'row'), may hold values from -1 to 1.2, as said below
Outputs:
- solution: float32 [64, 8, 1024], P('rhs', None, 'row'), parts along dimension 0
There are 2 independent parts, one for each index of `rhs`. A program takes and returns all parts, laid end to end along the dimension named above; an argument that names none is the same for every part. Nothing has to cross between parts.
Inputs may be any that keep to these rules, and one draw needn't show every extreme that they name: `inverse_blocks`: each block is lower triangular with diagonal entries between 0.5 and 1.2.
All inputs are finite; a program needn't handle non-finite values.
Results may differ from a plain program's by a relative error of at most 0.0001.
Values sent between devices are 32-bit elements; how exact they have to be, the bound alone decides.
A program may use at most 64 MiB of HBM per device.

v0:
```python
import jax
import jax.numpy as jnp
from jax import lax
from jax.sharding import PartitionSpec as P


def apply_rows(left, right):
    return lax.dot_general(
        left,
        right,
        (((1,), (1,)), ((), ())),
        precision=lax.Precision.HIGHEST,
        preferred_element_type=jnp.float32,
    )


def body(right_sides, lower_blocks, inverse_blocks):
    window = right_sides.shape[1]
    outputs = []
    solved = []
    for current in range(window):
        residual = right_sides[:, current, :]
        for earlier in range(current):
            index_pair = current * (current - 1) // 2 + earlier
            residual = residual - apply_rows(solved[earlier], lower_blocks[index_pair])
        inverse_now = inverse_blocks[current]
        local_rows = apply_rows(lax.all_gather(residual, "row", axis=1, tiled=True), inverse_now)
        full_solution = lax.all_gather(local_rows, "row", axis=1, tiled=True)
        full_solution, local_rows = (full_solution, local_rows)
        solved.append(full_solution)
        outputs.append(local_rows)
    return jnp.stack(outputs, axis=1)


def solution(mesh):
    return jax.shard_map(
        body,
        mesh=mesh,
        in_specs=(P("rhs", None, "row"), P(None, "row", None), P(None, "row", None)),
        out_specs=P("rhs", None, "row"),
        check_vma=False,
    )
```

profile of v0, /device:TPU:0, one launch (start us, length us, event | category | flops | bytes accessed | tf_op | source)
XLA Modules:
  0.0 625.1 jit_solution(15894234350832063314)
XLA Ops:
  0.0 1.9 fusion.87
  2.0 45.3 %all-gather = f32[32,1,1024]{0,1,2:T(1,128)S(1)} all-gather(f32[32,1,64]{0,1,2:T(1,128)S(1)} %copy.59), channel_id=2, replica_groups=mesh['row'=16,'rhs'=2] {'row'}, dimensions={2}, use_global_device_ids=true | all-gather | bytes 139264 | tf_op jit(solution)/shard_map/all_gather | solution.py:27
  47.3 1.9 constant_dynamic-update-slice_fusion.6
  49.2 36.9 %all-gather.1 = f32[16,64,32]{1,2,0:T(8,128)S(1)} all-gather(f32[1,64,32]{1,2,0:T(8,128)S(1)} %bitcast.277), channel_id=1, replica_groups=mesh['row'=16,'rhs'=2] {'row'}, dimensions={0}, use_global_device_ids=true | all-gather | bytes 139264 | tf_op jit(solution)/shard_map/all_gather | solution.py:28
  86.4 1.3 convolution_subtract_fusion.12
  87.6 1.3 convolution_subtract_fusion.17
  88.9 1.3 convolution_subtract_fusion.21
  90.2 1.3 convolution_subtract_fusion.24
  91.5 1.3 convolution_subtract_fusion.26
  92.8 1.3 fusion.7
  94.1 1.3 convolution_subtract_fusion.6
  95.4 38.9 %all-gather.2 = f32[16,64,32]{1,2,0:T(8,128)S(1)} all-gather(f32[1,64,32]{1,2,0:T(8,128)S(1)} %fusion.7), channel_id=1, replica_groups=mesh['row'=16,'rhs'=2] {'row'}, dimensions={0}, use_global_device_ids=true | all-gather | bytes 139264 | tf_op jit(solution)/shard_map/all_gather | solution.py:27
  134.6 1.3 constant_dynamic-update-slice_fusion.5
  135.9 37.1 %all-gather.3 = f32[16,64,32]{1,2,0:T(8,128)S(1)} all-gather(f32[1,64,32]{1,2,0:T(8,128)S(1)} %bitcast.285), channel_id=1, replica_groups=mesh['row'=16,'rhs'=2] {'row'}, dimensions={0}, use_global_device_ids=true | all-gather | bytes 139264 | tf_op jit(solution)/shard_map/all_gather | solution.py:28
  173.3 1.3 convolution_subtract_fusion.11
  174.6 1.3 convolution_subtract_fusion.16
  175.9 1.3 convolution_subtract_fusion.20
  177.2 1.3 convolution_subtract_fusion.23
  178.5 1.3 fusion.6
  179.8 1.3 convolution_subtract_fusion.5
  181.1 39.1 %all-gather.4 = f32[16,64,32]{1,2,0:T(8,128)S(1)} all-gather(f32[1,64,32]{1,2,0:T(8,128)S(1)} %fusion.6), channel_id=1, replica_groups=mesh['row'=16,'rhs'=2] {'row'}, dimensions={0}, use_global_device_ids=true | all-gather | bytes 139264 | tf_op jit(solution)/shard_map/all_gather | solution.py:27
  220.4 0.3 constant_dynamic-update-slice_fusion.4
  220.8 36.9 %all-gather.5 = f32[16,64,32]{1,2,0:T(8,128)S(1)} all-gather(f32[1,64,32]{1,2,0:T(8,128)S(1)} %bitcast.286), channel_id=1, replica_groups=mesh['row'=16,'rhs'=2] {'row'}, dimensions={0}, use_global_device_ids=true | all-gather | bytes 139264 | tf_op jit(solution)/shard_map/all_gather | solution.py:28
  257.9 1.3 convolution_subtract_fusion.10
  259.2 1.3 convolution_subtract_fusion.15
  260.5 1.3 convolution_subtract_fusion.19
  261.8 1.3 fusion.5
  263.1 1.3 convolution_subtract_fusion.4
  264.4 39.3 %all-gather.6 = f32[16,64,32]{1,2,0:T(8,128)S(1)} all-gather(f32[1,64,32]{1,2,0:T(8,128)S(1)} %fusion.5), channel_id=1, replica_groups=mesh['row'=16,'rhs'=2] {'row'}, dimensions={0}, use_global_device_ids=true | all-gather | bytes 139264 | tf_op jit(solution)/shard_map/all_gather | solution.py:27
  304.3 36.9 %all-gather.7 = f32[16,64,32]{1,2,0:T(8,128)S(1)} all-gather(f32[1,64,32]{1,2,0:T(8,128)S(1)} %bitcast.287), channel_id=1, replica_groups=mesh['row'=16,'rhs'=2] {'row'}, dimensions={0}, use_global_device_ids=true | all-gather | bytes 139264 | tf_op jit(solution)/shard_map/all_gather | solution.py:28
  341.5 1.3 convolution_subtract_fusion.9
  342.8 1.3 convolution_subtract_fusion.14
  344.1 1.3 fusion.4
  345.4 1.3 convolution_subtract_fusion.3
  346.7 39.0 %all-gather.8 = f32[16,64,32]{1,2,0:T(8,128)S(1)} all-gather(f32[1,64,32]{1,2,0:T(8,128)S(1)} %fusion.4), channel_id=1, replica_groups=mesh['row'=16,'rhs'=2] {'row'}, dimensions={0}, use_global_device_ids=true | all-gather | bytes 139264 | tf_op jit(solution)/shard_map/all_gather | solution.py:27
  386.3 36.9 %all-gather.9 = f32[16,64,32]{1,2,0:T(8,128)S(1)} all-gather(f32[1,64,32]{1,2,0:T(8,128)S(1)} %bitcast.288), channel_id=1, replica_groups=mesh['row'=16,'rhs'=2] {'row'}, dimensions={0}, use_global_device_ids=true | all-gather | bytes 139264 | tf_op jit(solution)/shard_map/all_gather | solution.py:28
  423.5 1.3 convolution_subtract_fusion.8
  424.8 1.3 fusion.3
  426.1 1.3 convolution_subtract_fusion.2
  427.4 38.9 %all-gather.10 = f32[16,64,32]{1,2,0:T(8,128)S(1)} all-gather(f32[1,64,32]{1,2,0:T(8,128)S(1)} %fusion.3), channel_id=1, replica_groups=mesh['row'=16,'rhs'=2] {'row'}, dimensions={0}, use_global_device_ids=true | all-gather | bytes 139264 | tf_op jit(solution)/shard_map/all_gather | solution.py:27
  466.9 37.2 %all-gather.11 = f32[16,64,32]{1,2,0:T(8,128)S(1)} all-gather(f32[1,64,32]{1,2,0:T(8,128)S(1)} %bitcast.289), channel_id=1, replica_groups=mesh['row'=16,'rhs'=2] {'row'}, dimensions={0}, use_global_device_ids=true | all-gather | bytes 139264 | tf_op jit(solution)/shard_map/all_gather | solution.py:28
  504.4 1.3 fusion.2
  505.7 1.3 convolution_subtract_fusion.1
  507.0 38.8 %all-gather.12 = f32[16,64,32]{1,2,0:T(8,128)S(1)} all-gather(f32[1,64,32]{1,2,0:T(8,128)S(1)} %fusion.2), channel_id=1, replica_groups=mesh['row'=16,'rhs'=2] {'row'}, dimensions={0}, use_global_device_ids=true | all-gather | bytes 139264 | tf_op jit(solution)/shard_map/all_gather | solution.py:27
  546.5 36.9 %all-gather.13 = f32[16,64,32]{1,2,0:T(8,128)S(1)} all-gather(f32[1,64,32]{1,2,0:T(8,128)S(1)} %bitcast.290), channel_id=1, replica_groups=mesh['row'=16,'rhs'=2] {'row'}, dimensions={0}, use_global_device_ids=true | all-gather | bytes 139264 | tf_op jit(solution)/shard_map/all_gather | solution.py:28
  583.6 1.3 fusion.1
  584.9 38.8 %all-gather.14 = f32[16,64,32]{1,2,0:T(8,128)S(1)} all-gather(f32[1,64,32]{1,2,0:T(8,128)S(1)} %fusion.1), channel_id=1, replica_groups=mesh['row'=16,'rhs'=2] {'row'}, dimensions={0}, use_global_device_ids=true | all-gather | bytes 139264 | tf_op jit(solution)/shard_map/all_gather | solution.py:27
  624.4 0.7 copy.58
  (36 shorter events, 5.7 us)
Async XLA Ops:
  0.0 220.4 %copy-start = (f32[8,64,1024]{2,1,0:T(8,128)S(1)}, f32[8,64,1024]{2,1,0:T(8,128)}, u32[]{:S(2)}) copy-start(f32[8,64,1024]{2,1,0:T(8,128)} %param.5) | copy-start | bytes 6291460
where the time goes:
time: 626 us; the launch traced here: 625 us
  blocking collectives  577 us (92%)
  matrix products  41.3 us (7%)
  local copies, waits for them, and re-layouts  6.65 us (1%)
    all_gather x8, blocking collectives, body(): lax.all_gather(residual, 'row', axis=1, tiled=True)  318 us
    all_gather x7, blocking collectives, body(): full_solution = lax.all_gather(local_rows, 'row', axis=1, tiled=True)  259 us
    dot_general x36, matrix products, apply_rows(): lax.dot_general(left, right, (((1,), (1,)), ((), ())), precision=lax.Prec...  41.3 us

commit v1 on v0

v1 whole, which is shorter than its diff:
```python
import functools

import jax
import jax.numpy as jnp
from jax import lax
from jax.experimental import pallas as pl
from jax.experimental.pallas import tpu as pltpu
from jax.sharding import PartitionSpec as P

MESH = pl.DeviceIdType.MESH
LANES = 128
PIECE = 16


def split(value):
    high = value.astype(jnp.bfloat16)
    low = (value - high.astype(jnp.float32)).astype(jnp.bfloat16)
    return high, low


def dot(left, right):
    return jnp.dot(left, right, preferred_element_type=jnp.float32)


def kernel(
    n, window, rhs, rows, b_ref, l_ref, inv_ref, o_ref,
    l_raw, inv_raw, l_hi, l_lo, inv_hi, inv_lo, held, x_hi, x_lo, total,
    l_sem, inv_sem, send_sem, recv_sem,
):
    me = lax.axis_index("row")
    fold = rows // PIECE

    inv_copies = []
    l_copies = []
    for j in range(window):
        copy = pltpu.make_async_copy(inv_ref.at[j], inv_raw.at[j], inv_sem.at[j])
        copy.start()
        inv_copies.append(copy)
        if j + 1 < window:
            k = j + 1
            part = pl.ds(k * (k - 1) // 2, k)
            copy = pltpu.make_async_copy(l_ref.at[part], l_raw.at[part], l_sem.at[j])
            copy.start()
            l_copies.append(copy)

    barrier = pltpu.get_barrier_semaphore()
    for d in range(1, n):
        pl.semaphore_signal(
            barrier, inc=1, device_id={"row": lax.rem(me + d, n)}, device_id_type=MESH
        )

    for j in range(window):
        mine = b_ref[:, j, :]
        mine = jnp.concatenate(
            [mine, jnp.zeros((LANES - rhs, rows), jnp.float32)], axis=0
        )
        total[j] = mine.T

    pl.semaphore_wait(barrier, n - 1)

    lane = lax.broadcasted_iota(jnp.int32, (PIECE, LANES), 1)

    def send(phase, value):
        piece = value[0:PIECE]
        for g in range(1, fold):
            moved = pltpu.roll(value[g * PIECE:(g + 1) * PIECE], g * rhs, 1)
            piece = jnp.where(lane < g * rhs, piece, moved)
        held[phase, me] = piece
        for d in range(1, n):
            pltpu.make_async_remote_copy(
                src_ref=held.at[phase, me],
                dst_ref=held.at[phase, me],
                send_sem=send_sem.at[phase],
                recv_sem=recv_sem.at[phase],
                device_id={"row": lax.rem(me + d, n)},
                device_id_type=MESH,
            ).start()

    def all_of(phase):
        part = held.at[phase, pl.ds(0, n - 1)]
        return pltpu.make_async_remote_copy(
            src_ref=part,
            dst_ref=part,
            send_sem=send_sem.at[phase],
            recv_sem=recv_sem.at[phase],
            device_id={"row": lax.rem(me + 1, n)},
            device_id_type=MESH,
        )

    def receive(phase):
        all_of(phase).wait_recv()
        for q in range(n):
            piece = held[phase, q]
            for g in range(fold):
                part = piece if g == 0 else pltpu.roll(piece, LANES - g * rhs, 1)
                high, low = split(part)
                at = q * rows + g * PIECE
                x_hi[at:at + PIECE, :] = high
                x_lo[at:at + PIECE, :] = low

    def apply(high, low):
        return dot(high, x_hi[...]) + dot(low, x_hi[...]) + dot(high, x_lo[...])

    def pair(j, i):
        return j * (j - 1) // 2 + i

    for j in range(window):
        send(2 * j, total[j])
        inv_copies[j].wait()
        inv_hi[j], inv_lo[j] = split(inv_raw[j])
        if j + 1 < window:
            if j < 2:
                l_copies[j].wait()
            l_hi[j], l_lo[j] = split(l_raw[pair(j + 1, j)])
        if j > 0:
            for k in range(j + 1, window):
                if j == 1 and k > j + 1:
                    l_copies[k - 1].wait()
                high, low = split(l_raw[pair(k, j - 1)])
                total[k] = total[k] - apply(high, low)
        receive(2 * j)
        value = apply(inv_hi[j], inv_lo[j])
        if j + 1 < window:
            send(2 * j + 1, value)
        o_ref[:, j, :] = value.T[0:rhs]
        if j + 1 < window:
            receive(2 * j + 1)
            total[j + 1] = total[j + 1] - apply(l_hi[j], l_lo[j])

    for phase in range(2 * window - 1):
        all_of(phase).wait_send()


def body(right_sides, lower_blocks, inverse_blocks):
    n = lax.axis_size("row")
    rhs, window, rows = right_sides.shape
    pairs, _, size = lower_blocks.shape
    phases = 2 * window - 1
    return pl.pallas_call(
        functools.partial(kernel, n, window, rhs, rows),
        out_shape=jax.ShapeDtypeStruct(right_sides.shape, jnp.float32),
        in_specs=[
            pl.BlockSpec(memory_space=pltpu.VMEM),
            pl.BlockSpec(memory_space=pl.ANY),
            pl.BlockSpec(memory_space=pl.ANY),
        ],
        out_specs=pl.BlockSpec(memory_space=pltpu.VMEM),
        scratch_shapes=[
            pltpu.VMEM((pairs, rows, size), jnp.float32),
            pltpu.VMEM((window, rows, size), jnp.float32),
            pltpu.VMEM((window, rows, size), jnp.bfloat16),
            pltpu.VMEM((window, rows, size), jnp.bfloat16),
            pltpu.VMEM((window, rows, size), jnp.bfloat16),
            pltpu.VMEM((window, rows, size), jnp.bfloat16),
            pltpu.VMEM((phases, n, PIECE, LANES), jnp.float32),
            pltpu.VMEM((size, LANES), jnp.bfloat16),
            pltpu.VMEM((size, LANES), jnp.bfloat16),
            pltpu.VMEM((window, rows, LANES), jnp.float32),
            pltpu.SemaphoreType.DMA((window,)),
            pltpu.SemaphoreType.DMA((window,)),
            pltpu.SemaphoreType.DMA((phases,)),
            pltpu.SemaphoreType.DMA((phases,)),
        ],
        compiler_params=pltpu.CompilerParams(
            collective_id=0, has_side_effects=True, vmem_limit_bytes=40 << 20
        ),
    )(right_sides, lower_blocks, inverse_blocks)


def solution(mesh):
    return jax.shard_map(
        body,
        mesh=mesh,
        in_specs=(P("rhs", None, "row"), P(None, "row", None), P(None, "row", None)),
        out_specs=P("rhs", None, "row"),
        check_vma=False,
    )
```

time: 626 us -> 98.6 us (0.16)
  blocking collectives: 577 us -> 0 us
  Pallas kernels: 0 us -> 92.1 us
  matrix products: 41.3 us -> 0 us
    all_gather x15 -> x0, blocking collectives: 577 us -> none  [the longest x8 318 us: body(): lax.all_gather(residual, 'row', axis=1, tiled=True)]
    pallas_call x0 -> x1, Pallas kernels: none -> 92.1 us  [body(): pl.pallas_call(functools.partial(kernel, n, window, rhs, rows), out_shape...]
    dot_general x36 -> x0, matrix products: 41.3 us -> none  [apply_rows(): lax.dot_general(left, right, (((1,), (1,)), ((), ())), precision=lax.Prec...]
where the time goes in v1:
time: 98.6 us; the launch traced here: 98.4 us
  Pallas kernels  92.1 us (93%)
  local copies, waits for them, and re-layouts  6.23 us (6%)
    pallas_call x1, Pallas kernels, body(): pl.pallas_call(functools.partial(kernel, n, window, rhs, rows), out_shape...  92.1 us
    unnamed x7, local copies, waits for them, and re-layouts  6.23 us

profile of v1, /device:TPU:0, one launch (start us, length us, event | category | flops | bytes accessed | tf_op | source)
XLA Modules:
  0.0 98.4 jit_solution(7756129943303176862)
XLA Ops:
  0.0 0.0 copy-start
  0.0 3.1 %copy-done = f32[28,64,1024]{2,1,0:T(8,128)S(1)} copy-done((f32[28,64,1024]{2,1,0:T(8,128)S(1)}, f32[28,64,1024]{2,1,0:T(8,128)}, u32[]{:S(2)}) %copy-start) | copy-done | bytes 7340056
  3.1 0.0 copy-start.1
  3.1 1.6 %copy-done.1 = f32[8,64,1024]{2,1,0:T(8,128)S(1)} copy-done((f32[8,64,1024]{2,1,0:T(8,128)S(1)}, f32[8,64,1024]{2,1,0:T(8,128)}, u32[]{:S(2)}) %copy-start.1) | copy-done | bytes 2097176
  4.7 0.0 copy-start.2
  4.7 0.9 copy-done.2
  5.6 92.1 %shard_map.37 = f32[32,8,64]{2,1,0:T(8,128)S(1)} custom-call(f32[32,8,64]{2,1,0:T(8,128)S(1)} %copy-done.2, f32[28,64,1024]{2,1,0:T(8,128)S(1)} %copy-done, f32[8,64,1024]{2,1,0:T(8,128)S(1)} %copy-done.1), custom_call_target="tpu_custom_call" | custom-call | tf_op jit(solution)/shard_map/pallas_call | solution.py:139
  97.7 0.7 copy.5
Async XLA Ops:
  0.0 3.1 %copy-start = (f32[28,64,1024]{2,1,0:T(8,128)S(1)}, f32[28,64,1024]{2,1,0:T(8,128)}, u32[]{:S(2)}) copy-start(f32[28,64,1024]{2,1,0:T(8,128)} %l_ref.1) | copy-start | bytes 22020100
  3.1 1.6 %copy-start.1 = (f32[8,64,1024]{2,1,0:T(8,128)S(1)}, f32[8,64,1024]{2,1,0:T(8,128)}, u32[]{:S(2)}) copy-start(f32[8,64,1024]{2,1,0:T(8,128)} %inv_ref.1) | copy-start | bytes 6291460
  4.7 0.9 copy-start.2

commit v2 on v1

--- a/solution.py
+++ b/solution.py
@@ -10,6 +10,7 @@
 MESH = pl.DeviceIdType.MESH
 LANES = 128
 PIECE = 16
+CHUNK = 256
 
 
 def split(value):
@@ -29,6 +30,9 @@
 ):
     me = lax.axis_index("row")
     fold = rows // PIECE
+    group = CHUNK // rows
+    groups = n // group
+    mine, place = me // group, lax.rem(me, group)
 
     inv_copies = []
     l_copies = []
@@ -50,13 +54,20 @@
         )
 
     for j in range(window):
-        mine = b_ref[:, j, :]
-        mine = jnp.concatenate(
-            [mine, jnp.zeros((LANES - rhs, rows), jnp.float32)], axis=0
+        part = b_ref[:, j, :]
+        part = jnp.concatenate(
+            [part, jnp.zeros((LANES - rhs, rows), jnp.float32)], axis=0
         )
-        total[j] = mine.T
+        total[j] = part.T
 
     pl.semaphore_wait(barrier, n - 1)
+
+    def partner(d):
+        if groups != 4:
+            return lax.rem(mine + d, groups)
+        if d == 1:
+            return mine + 1 - 2 * lax.rem(mine, 2)
+        return (mine, None, lax.rem(mine + 2, 4), 3 - mine)[d]
 
     lane = lax.broadcasted_iota(jnp.int32, (PIECE, LANES), 1)
 
@@ -66,40 +77,67 @@
             moved = pltpu.roll(value[g * PIECE:(g + 1) * PIECE], g * rhs, 1)
             piece = jnp.where(lane < g * rhs, piece, moved)
         held[phase, me] = piece
-        for d in range(1, n):
-            pltpu.make_async_remote_copy(
-                src_ref=held.at[phase, me],
-                dst_ref=held.at[phase, me],
-                send_sem=send_sem.at[phase],
-                recv_sem=recv_sem.at[phase],
-                device_id={"row": lax.rem(me + d, n)},
-                device_id_type=MESH,
-            ).start()
-
-    def all_of(phase):
-        part = held.at[phase, pl.ds(0, n - 1)]
+        for d in reversed(range(groups)):
+            other = partner(d)
+            for e in reversed(range(group)):
+                if d == 0 and e == 0:
+                    continue
+                target = other * group + lax.rem(place + e, group)
+                pltpu.make_async_remote_copy(
+                    src_ref=held.at[phase, me],
+                    dst_ref=held.at[phase, me],
+                    send_sem=send_sem.at[phase],
+                    recv_sem=recv_sem.at[phase, mine],
+                    device_id={"row": target},
+                    device_id_type=MESH,
+                ).start()
+
+    def all_of(phase, source, count):
+        part = held.at[phase, pl.ds(0, count)]
         return pltpu.make_async_remote_copy(
             src_ref=part,
             dst_ref=part,
             send_sem=send_sem.at[phase],
-            recv_sem=recv_sem.at[phase],
+            recv_sem=recv_sem.at[phase, source],
             device_id={"row": lax.rem(me + 1, n)},
             device_id_type=MESH,
         )
 
-    def receive(phase):
-        all_of(phase).wait_recv()
-        for q in range(n):
-            piece = held[phase, q]
-            for g in range(fold):
-                part = piece if g == 0 else pltpu.roll(piece, LANES - g * rhs, 1)
-                high, low = split(part)
-                at = q * rows + g * PIECE
-                x_hi[at:at + PIECE, :] = high
-                x_lo[at:at + PIECE, :] = low
+    def receive(phase, high, low):
+        side = phase % 2
+        result = None
+        for d in range(groups):
+            source = partner(d)
+            all_of(phase, source, group - 1 if d == 0 else group).wait_recv()
+            highs, lows = [], []
+            for k in range(group):
+                piece = held[phase, source * group + k]
+                for g in range(fold):
+                    part = piece if g == 0 else pltpu.roll(piece, LANES - g * rhs, 1)
+                    one, two = split(part)
+                    highs.append(one)
+                    lows.append(two)
+            right_high = jnp.concatenate(highs, axis=0)
+            right_low = jnp.concatenate(lows, axis=0)
+            at = pl.ds(pl.multiple_of(source * CHUNK, CHUNK), CHUNK)
+            if side:
+                x_hi[at, :] = right_high
+                x_lo[at, :] = right_low
+            left_high, left_low = high[:, at], low[:, at]
+            term = dot(left_high, right_high) + dot(left_low, right_high)
+            term = term + dot(left_high, right_low)
+            result = term if result is None else result + term
+        return result
 
     def apply(high, low):
         return dot(high, x_hi[...]) + dot(low, x_hi[...]) + dot(high, x_lo[...])
+
+    def older(j, first, last):
+        for k in range(first, last):
+            if j == 1:
+                l_copies[k - 1].wait()
+            high, low = split(l_raw[pair(k, j - 1)])
+            total[k] = total[k] - apply(high, low)
 
     def pair(j, i):
         return j * (j - 1) // 2 + i
@@ -108,27 +146,23 @@
         send(2 * j, total[j])
         inv_copies[j].wait()
         inv_hi[j], inv_lo[j] = split(inv_raw[j])
-        if j + 1 < window:
-            if j < 2:
-                l_copies[j].wait()
-            l_hi[j], l_lo[j] = split(l_raw[pair(j + 1, j)])
+        middle = j + 1 + (window - j) // 2
         if j > 0:
-            for k in range(j + 1, window):
-                if j == 1 and k > j + 1:
-                    l_copies[k - 1].wait()
-                high, low = split(l_raw[pair(k, j - 1)])
-                total[k] = total[k] - apply(high, low)
-        receive(2 * j)
-        value = apply(inv_hi[j], inv_lo[j])
+            older(j, j + 1, min(middle, window))
+        value = receive(2 * j, inv_hi.at[j], inv_lo.at[j])
         if j + 1 < window:
             send(2 * j + 1, value)
         o_ref[:, j, :] = value.T[0:rhs]
         if j + 1 < window:
-            receive(2 * j + 1)
-            total[j + 1] = total[j + 1] - apply(l_hi[j], l_lo[j])
+            if j == 0:
+                l_copies[j].wait()
+            l_hi[j], l_lo[j] = split(l_raw[pair(j + 1, j)])
+            if j > 0:
+                older(j, middle, window)
+            total[j + 1] = total[j + 1] - receive(2 * j + 1, l_hi.at[j], l_lo.at[j])
 
     for phase in range(2 * window - 1):
-        all_of(phase).wait_send()
+        all_of(phase, 0, n - 1).wait_send()
 
 
 def body(right_sides, lower_blocks, inverse_blocks):
@@ -159,7 +193,7 @@
             pltpu.SemaphoreType.DMA((window,)),
             pltpu.SemaphoreType.DMA((window,)),
             pltpu.SemaphoreType.DMA((phases,)),
-            pltpu.SemaphoreType.DMA((phases,)),
+            pltpu.SemaphoreType.DMA((phases, n * rows // CHUNK)),
         ],
         compiler_params=pltpu.CompilerParams(
             collective_id=0, has_side_effects=True, vmem_limit_bytes=40 << 20

time: 98.6 us -> 99.5 us (level)
  Pallas kernels: 92.1 us -> 93.1 us
where the time goes in v2:
time: 99.5 us; the launch traced here: 99.3 us
  Pallas kernels  93.1 us (94%)
  local copies, waits for them, and re-layouts  6.23 us (6%)
    pallas_call x1, Pallas kernels, body(): pl.pallas_call(functools.partial(kernel, n, window, rhs, rows), out_shape...  93.1 us
    unnamed x7, local copies, waits for them, and re-layouts  6.23 us

profile of v2, /device:TPU:0, one launch (start us, length us, event | category | flops | bytes accessed | tf_op | source)
XLA Modules:
  0.0 99.3 jit_solution(17127295076769845169)
XLA Ops:
  0.0 0.0 copy-start
  0.0 3.1 %copy-done = f32[28,64,1024]{2,1,0:T(8,128)S(1)} copy-done((f32[28,64,1024]{2,1,0:T(8,128)S(1)}, f32[28,64,1024]{2,1,0:T(8,128)}, u32[]{:S(2)}) %copy-start) | copy-done | bytes 7340056
  3.1 0.0 copy-start.1
  3.1 1.6 %copy-done.1 = f32[8,64,1024]{2,1,0:T(8,128)S(1)} copy-done((f32[8,64,1024]{2,1,0:T(8,128)S(1)}, f32[8,64,1024]{2,1,0:T(8,128)}, u32[]{:S(2)}) %copy-start.1) | copy-done | bytes 2097176
  4.7 0.0 copy-start.2
  4.7 0.9 copy-done.2
  5.6 93.1 %shard_map.37 = f32[32,8,64]{2,1,0:T(8,128)S(1)} custom-call(f32[32,8,64]{2,1,0:T(8,128)S(1)} %copy-done.2, f32[28,64,1024]{2,1,0:T(8,128)S(1)} %copy-done, f32[8,64,1024]{2,1,0:T(8,128)S(1)} %copy-done.1), custom_call_target="tpu_custom_call" | custom-call | tf_op jit(solution)/shard_map/pallas_call | solution.py:173
  98.7 0.7 copy.5
Async XLA Ops:
  0.0 3.1 %copy-start = (f32[28,64,1024]{2,1,0:T(8,128)S(1)}, f32[28,64,1024]{2,1,0:T(8,128)}, u32[]{:S(2)}) copy-start(f32[28,64,1024]{2,1,0:T(8,128)} %l_ref.1) | copy-start | bytes 22020100
  3.1 1.6 %copy-start.1 = (f32[8,64,1024]{2,1,0:T(8,128)S(1)}, f32[8,64,1024]{2,1,0:T(8,128)}, u32[]{:S(2)}) copy-start(f32[8,64,1024]{2,1,0:T(8,128)} %inv_ref.1) | copy-start | bytes 6291460
  4.7 0.9 copy-start.2

commit v3 on v2

--- a/solution.py
+++ b/solution.py
@@ -60,6 +60,14 @@
         )
         total[j] = part.T
 
+    for later in range(1, groups):
+        @pl.when(later > mine)
+        def _(later=later):
+            for j in range(window):
+                held[2 * j, later * group:(later + 1) * group] = jnp.zeros(
+                    (group, PIECE, LANES), jnp.float32
+                )
+
     pl.semaphore_wait(barrier, n - 1)
 
     def partner(d):
@@ -79,25 +87,31 @@
         held[phase, me] = piece
         for d in reversed(range(groups)):
             other = partner(d)
-            for e in reversed(range(group)):
-                if d == 0 and e == 0:
-                    continue
-                target = other * group + lax.rem(place + e, group)
-                pltpu.make_async_remote_copy(
-                    src_ref=held.at[phase, me],
-                    dst_ref=held.at[phase, me],
-                    send_sem=send_sem.at[phase],
-                    recv_sem=recv_sem.at[phase, mine],
-                    device_id={"row": target},
-                    device_id_type=MESH,
-                ).start()
-
-    def all_of(phase, source, count):
-        part = held.at[phase, pl.ds(0, count)]
+
+            def to_group(d=d, other=other):
+                for e in reversed(range(group)):
+                    if d == 0 and e == 0:
+                        continue
+                    pltpu.make_async_remote_copy(
+                        src_ref=held.at[phase, me],
+                        dst_ref=held.at[phase, me],
+                        send_sem=send_sem.at[phase, d],
+                        recv_sem=recv_sem.at[phase, mine],
+                        device_id={"row": other * group + lax.rem(place + e, group)},
+                        device_id_type=MESH,
+                    ).start()
+
+            if d == 0 or phase % 2:
+                to_group()
+            else:
+                pl.when(other > mine)(to_group)
+
+    def all_of(phase, source, d):
+        part = held.at[phase, pl.ds(0, group - 1 if d == 0 else group)]
         return pltpu.make_async_remote_copy(
             src_ref=part,
             dst_ref=part,
-            send_sem=send_sem.at[phase],
+            send_sem=send_sem.at[phase, d],
             recv_sem=recv_sem.at[phase, source],
             device_id={"row": lax.rem(me + 1, n)},
             device_id_type=MESH,
@@ -105,10 +119,16 @@
 
     def receive(phase, high, low):
         side = phase % 2
+        for d in range(groups):
+            source = partner(d)
+            copies = all_of(phase, source, d)
+            if d == 0 or side:
+                copies.wait_recv()
+            else:
+                pl.when(source < mine)(copies.wait_recv)
         result = None
         for d in range(groups):
             source = partner(d)
-            all_of(phase, source, group - 1 if d == 0 else group).wait_recv()
             highs, lows = [], []
             for k in range(group):
                 piece = held[phase, source * group + k]
@@ -162,7 +182,13 @@
             total[j + 1] = total[j + 1] - receive(2 * j + 1, l_hi.at[j], l_lo.at[j])
 
     for phase in range(2 * window - 1):
-        all_of(phase, 0, n - 1).wait_send()
+        for d in range(groups):
+            other = partner(d)
+            copies = all_of(phase, other, d)
+            if d == 0 or phase % 2:
+                copies.wait_send()
+            else:
+                pl.when(other > mine)(copies.wait_send)
 
 
 def body(right_sides, lower_blocks, inverse_blocks):
@@ -192,7 +218,7 @@
             pltpu.VMEM((window, rows, LANES), jnp.float32),
             pltpu.SemaphoreType.DMA((window,)),
             pltpu.SemaphoreType.DMA((window,)),
-            pltpu.SemaphoreType.DMA((phases,)),
+            pltpu.SemaphoreType.DMA((phases, n * rows // CHUNK)),
             pltpu.SemaphoreType.DMA((phases, n * rows // CHUNK)),
         ],
         compiler_params=pltpu.CompilerParams(

time: 99.5 us -> 93.6 us (0.941)
  Pallas kernels: 93.1 us -> 87.2 us
    pallas_call x1, Pallas kernels: 93.1 us -> 87.2 us  [body(): pl.pallas_call(functools.partial(kernel, n, window, rhs, rows), out_shape...]
where the time goes in v3:
time: 93.6 us; the launch traced here: 93.4 us
  Pallas kernels  87.2 us (93%)
  local copies, waits for them, and re-layouts  6.23 us (7%)
    pallas_call x1, Pallas kernels, body(): pl.pallas_call(functools.partial(kernel, n, window, rhs, rows), out_shape...  87.2 us
    unnamed x7, local copies, waits for them, and re-layouts  6.23 us

profile of v3, /device:TPU:0, one launch (start us, length us, event | category | flops | bytes accessed | tf_op | source)
XLA Modules:
  0.0 93.4 jit_solution(2538884283001797134)
XLA Ops:
  0.0 0.0 copy-start
  0.0 3.1 %copy-done = f32[28,64,1024]{2,1,0:T(8,128)S(1)} copy-done((f32[28,64,1024]{2,1,0:T(8,128)S(1)}, f32[28,64,1024]{2,1,0:T(8,128)}, u32[]{:S(2)}) %copy-start) | copy-done | bytes 7340056
  3.1 0.0 copy-start.1
  3.1 1.6 %copy-done.1 = f32[8,64,1024]{2,1,0:T(8,128)S(1)} copy-done((f32[8,64,1024]{2,1,0:T(8,128)S(1)}, f32[8,64,1024]{2,1,0:T(8,128)}, u32[]{:S(2)}) %copy-start.1) | copy-done | bytes 2097176
  4.7 0.0 copy-start.2
  4.7 0.9 copy-done.2
  5.6 87.2 %shard_map.37 = f32[32,8,64]{2,1,0:T(8,128)S(1)} custom-call(f32[32,8,64]{2,1,0:T(8,128)S(1)} %copy-done.2, f32[28,64,1024]{2,1,0:T(8,128)S(1)} %copy-done, f32[8,64,1024]{2,1,0:T(8,128)S(1)} %copy-done.1), custom_call_target="tpu_custom_call" | custom-call | tf_op jit(solution)/shard_map/pallas_call | solution.py:199
  92.7 0.7 copy.5
Async XLA Ops:
  0.0 3.1 %copy-start = (f32[28,64,1024]{2,1,0:T(8,128)S(1)}, f32[28,64,1024]{2,1,0:T(8,128)}, u32[]{:S(2)}) copy-start(f32[28,64,1024]{2,1,0:T(8,128)} %l_ref.1) | copy-start | bytes 22020100
  3.1 1.6 %copy-start.1 = (f32[8,64,1024]{2,1,0:T(8,128)S(1)}, f32[8,64,1024]{2,1,0:T(8,128)}, u32[]{:S(2)}) copy-start(f32[8,64,1024]{2,1,0:T(8,128)} %inv_ref.1) | copy-start | bytes 6291460
  4.7 0.9 copy-start.2

commit v4 on v3

--- a/solution.py
+++ b/solution.py
@@ -119,15 +119,21 @@
 
     def receive(phase, high, low):
         side = phase % 2
-        for d in range(groups):
+        def arrive(d):
             source = partner(d)
             copies = all_of(phase, source, d)
             if d == 0 or side:
                 copies.wait_recv()
             else:
                 pl.when(source < mine)(copies.wait_recv)
+
+        arrive(0)
+        arrive(1)
         result = None
         for d in range(groups):
+            if d == 2:
+                arrive(2)
+                arrive(3)
             source = partner(d)
             highs, lows = [], []
             for k in range(group):
@@ -144,8 +150,8 @@
                 x_hi[at, :] = right_high
                 x_lo[at, :] = right_low
             left_high, left_low = high[:, at], low[:, at]
-            term = dot(left_high, right_high) + dot(left_low, right_high)
-            term = term + dot(left_high, right_low)
+            both = dot(jnp.concatenate([left_high, left_low], axis=0), right_high)
+            term = both[:rows] + both[rows:] + dot(left_high, right_low)
             result = term if result is None else result + term
         return result
 

time: 93.6 us -> 92.3 us (0.986)
  Pallas kernels: 87.2 us -> 85.9 us
    pallas_call x1, Pallas kernels: 87.2 us -> 85.9 us  [body(): pl.pallas_call(functools.partial(kernel, n, window, rhs, rows), out_shape...]
where the time goes in v4:
time: 92.3 us; the launch traced here: 92.1 us
  Pallas kernels  85.9 us (93%)
  local copies, waits for them, and re-layouts  6.23 us (7%)
    pallas_call x1, Pallas kernels, body(): pl.pallas_call(functools.partial(kernel, n, window, rhs, rows), out_shape...  85.9 us
    unnamed x7, local copies, waits for them, and re-layouts  6.23 us

profile of v4, /device:TPU:0, one launch (start us, length us, event | category | flops | bytes accessed | tf_op | source)
XLA Modules:
  0.0 92.1 jit_solution(16225480529067662021)
XLA Ops:
  0.0 0.0 copy-start
  0.0 3.1 %copy-done = f32[28,64,1024]{2,1,0:T(8,128)S(1)} copy-done((f32[28,64,1024]{2,1,0:T(8,128)S(1)}, f32[28,64,1024]{2,1,0:T(8,128)}, u32[]{:S(2)}) %copy-start) | copy-done | bytes 7340056
  3.1 0.0 copy-start.1
  3.1 1.6 %copy-done.1 = f32[8,64,1024]{2,1,0:T(8,128)S(1)} copy-done((f32[8,64,1024]{2,1,0:T(8,128)S(1)}, f32[8,64,1024]{2,1,0:T(8,128)}, u32[]{:S(2)}) %copy-start.1) | copy-done | bytes 2097176
  4.7 0.0 copy-start.2
  4.7 0.9 copy-done.2
  5.6 85.9 %shard_map.37 = f32[32,8,64]{2,1,0:T(8,128)S(1)} custom-call(f32[32,8,64]{2,1,0:T(8,128)S(1)} %copy-done.2, f32[28,64,1024]{2,1,0:T(8,128)S(1)} %copy-done, f32[8,64,1024]{2,1,0:T(8,128)S(1)} %copy-done.1), custom_call_target="tpu_custom_call" | custom-call | tf_op jit(solution)/shard_map/pallas_call | solution.py:205
  91.5 0.7 copy.5
Async XLA Ops:
  0.0 3.1 %copy-start = (f32[28,64,1024]{2,1,0:T(8,128)S(1)}, f32[28,64,1024]{2,1,0:T(8,128)}, u32[]{:S(2)}) copy-start(f32[28,64,1024]{2,1,0:T(8,128)} %l_ref.1) | copy-start | bytes 22020100
  3.1 1.6 %copy-start.1 = (f32[8,64,1024]{2,1,0:T(8,128)S(1)}, f32[8,64,1024]{2,1,0:T(8,128)}, u32[]{:S(2)}) copy-start(f32[8,64,1024]{2,1,0:T(8,128)} %inv_ref.1) | copy-start | bytes 6291460
  4.7 0.9 copy-start.2
